TPU v7x, 32 devices: a whole 2x2x4 slice. The times are simulated.
32 devices in a mesh: row: 16 (over z, x, core), col: 2 (over y).
Axes of the slice: x: 2, y: 2, z: 4, core: 2. Of those that a mesh axis runs over, the one named last changes fastest.
Arguments:
- first_homolog_embedding: bfloat16 [128, 512, 32], P(None, ('row', 'col')), may hold values from -12 to 12
- second_homolog_embedding: bfloat16 [128, 512, 32], P(None, ('row', 'col')), may hold values from -12 to 12
- token_chain_index: int32 [512], replicated, may hold values from 0 to 7, never falling along the last dimension, each value on 1 to 192 neighbouring positions
- incoming_pair_state: bfloat16 [512, 512, 128], P('row', 'col'), may hold values from -6 to 6
- tensor_mixing_matrix: bfloat16 [1024, 128], replicated, may hold values from -0.1875 to 0.1875
- outer_product_bias: float32 [128], replicated, may hold values from -3 to 3
- transition_norm_gain: float32 [128], replicated, may hold values from 0.5 to 1.5
- transition_gate_weight: bfloat16 [128, 512], replicated, may hold values from -0.5 to 0.5
- transition_up_weight: bfloat16 [128, 512], replicated, may hold values from -0.5 to 0.5
- transition_down_weight: bfloat16 [512, 128], replicated, may hold values from -0.25 to 0.25
- distogram_weight: bfloat16 [128, 64], replicated, may hold values from -0.5 to 0.5
- distogram_bias: float32 [64], replicated, may hold values from -3 to 3
Outputs:
- pair_out: bfloat16 [512, 512, 128], P('row', 'col')
- logits: float32 [64, 512, 512], P(None, 'row', 'col')
Inputs may be any that keep to these rules, and one draw needn't show every extreme that they name: `token_chain_index`: chain numbers never fall along the tokens; each chain has 1 to 192 tokens and one chain has exactly 192.
All inputs are finite; a program needn't handle non-finite values.
Results may differ from a plain program's by a relative error of at most 0.006.
Values may be sent and summed in bfloat16 or wider, within the bound.
A program may use at most 64 MiB of HBM per device.

v0:
```python
import jax
import jax.numpy as jnp
from jax import lax
from jax.sharding import PartitionSpec as P


def layer_norm(values, transition_norm_gain):
    center = jnp.mean(values, axis=-1, keepdims=True)
    shifted = values - center
    spread = jnp.mean(shifted * shifted, axis=-1, keepdims=True)
    return shifted * lax.rsqrt(spread + 1e-05) * transition_norm_gain


def transition_rows(
    mid_rows,
    transition_norm_gain,
    transition_gate_weight,
    transition_up_weight,
    transition_down_weight,
):
    mid_float = mid_rows.astype(jnp.float32)
    normed = layer_norm(mid_float, transition_norm_gain).astype(jnp.bfloat16)
    gate_pre = jnp.dot(normed, transition_gate_weight, preferred_element_type=jnp.float32)
    up_pre = jnp.dot(normed, transition_up_weight, preferred_element_type=jnp.float32)
    hidden = (jax.nn.silu(gate_pre) * up_pre).astype(jnp.bfloat16)
    result = mid_float + jnp.dot(hidden, transition_down_weight, preferred_element_type=jnp.float32)
    return result.astype(jnp.bfloat16)


def transition_tile(
    mid_tile,
    transition_norm_gain,
    transition_gate_weight,
    transition_up_weight,
    transition_down_weight,
):
    tile_shape = mid_tile.shape
    rows_all = tile_shape[0] * tile_shape[1]
    grid_piece = min(512, rows_all)
    blocks = mid_tile.reshape(rows_all // grid_piece, grid_piece, tile_shape[2])

    def one_block(rows):
        return transition_rows(
            rows,
            transition_norm_gain,
            transition_gate_weight,
            transition_up_weight,
            transition_down_weight,
        )

    return lax.map(one_block, blocks).reshape(tile_shape)


def mirror_tile(pair_tile):
    row_count = lax.axis_size("row")
    col_count = lax.axis_size("col")
    rows_tile, cols_tile, channels = pair_tile.shape
    row_groups = row_count // col_count
    step_two = lax.all_to_all(
        lax.all_to_all(pair_tile, "col", split_axis=0, concat_axis=1, tiled=True),
        "row",
        split_axis=1,
        concat_axis=0,
        tiled=True,
    )
    regrouped = step_two.reshape(col_count, row_groups, rows_tile // col_count, rows_tile, channels)
    step_three = lax.all_to_all(regrouped, "col", split_axis=0, concat_axis=2, tiled=True)
    return step_three.reshape(cols_tile, rows_tile, channels)


def per_device(
    first_homolog_embedding,
    second_homolog_embedding,
    token_chain_index,
    incoming_pair_state,
    tensor_mixing_matrix,
    outer_product_bias,
    transition_norm_gain,
    transition_gate_weight,
    transition_up_weight,
    transition_down_weight,
    distogram_weight,
    distogram_bias,
):
    row_count = lax.axis_size("row")
    col_count = lax.axis_size("col")
    row_at = lax.axis_index("row")
    col_at = lax.axis_index("col")
    rows_tile, cols_tile, channels = incoming_pair_state.shape
    sequence_total_count = first_homolog_embedding.shape[0]
    alignment_slab_length = sequence_total_count // 2
    projection_width = first_homolog_embedding.shape[2]
    tokens_local = first_homolog_embedding.shape[1]
    left_sequence_rows = lax.all_gather(first_homolog_embedding, "col", axis=1, tiled=True)
    relaid = lax.all_to_all(
        lax.all_to_all(second_homolog_embedding, "row", split_axis=0, concat_axis=1, tiled=True),
        "col",
        split_axis=1,
        concat_axis=1,
        tiled=True,
    )
    row_groups = row_count // col_count
    relaid = relaid.reshape(
        sequence_total_count // row_count, col_count, row_groups, tokens_local, projection_width
    )
    relaid = jnp.transpose(relaid, (0, 2, 1, 3, 4)).reshape(
        sequence_total_count // row_count, cols_tile, projection_width
    )
    right_cols = lax.all_gather(relaid, "row", axis=0, tiled=True)
    chain_rows = lax.dynamic_slice_in_dim(token_chain_index, row_at * rows_tile, rows_tile, 0)
    chain_cols = lax.dynamic_slice_in_dim(token_chain_index, col_at * cols_tile, cols_tile, 0)
    same_chain = (chain_rows[:, None] == chain_cols[None, :]).astype(jnp.float32)
    block_rows = max(1, min(rows_tile, 512 // cols_tile))
    block_count = rows_tile // block_rows
    paired_right = right_cols[:alignment_slab_length]
    unpaired_right = right_cols[alignment_slab_length:]

    def outer_block(block_index):
        row_start = block_index * block_rows
        left_block = lax.dynamic_slice_in_dim(left_sequence_rows, row_start, block_rows, 1)
        chain_mask = lax.dynamic_slice_in_dim(same_chain, row_start, block_rows, 0)
        paired_sum = jnp.einsum(
            "sic,sjd->ijcd",
            left_block[:alignment_slab_length],
            paired_right,
            preferred_element_type=jnp.float32,
        )

        def unpaired_terms():
            return jnp.einsum(
                "sic,sjd->ijcd",
                left_block[alignment_slab_length:],
                unpaired_right,
                preferred_element_type=jnp.float32,
            )

        def no_terms():
            return jnp.zeros_like(paired_sum)

        unpaired_sum = lax.cond(jnp.any(chain_mask > 0.5), unpaired_terms, no_terms)
        weight = chain_mask[:, :, None, None]
        homolog_mean = (paired_sum + weight * unpaired_sum) / (
            alignment_slab_length * (1.0 + weight)
        )
        raveled_matrix = homolog_mean.astype(jnp.bfloat16).reshape(
            block_rows * cols_tile, projection_width * projection_width
        )
        inputs = lax.dynamic_slice_in_dim(incoming_pair_state, row_start, block_rows, 0).reshape(
            block_rows * cols_tile, channels
        )
        middle = jnp.dot(raveled_matrix, tensor_mixing_matrix, preferred_element_type=jnp.float32)
        middle = middle + outer_product_bias + inputs.astype(jnp.float32)
        return middle.astype(jnp.bfloat16).reshape(block_rows, cols_tile, channels)

    pair_mid = lax.map(outer_block, jnp.arange(block_count, dtype=jnp.int32)).reshape(
        rows_tile, cols_tile, channels
    )
    pair_out = transition_tile(
        pair_mid,
        transition_norm_gain,
        transition_gate_weight,
        transition_up_weight,
        transition_down_weight,
    )
    mirror_out = mirror_tile(pair_out)
    own_bins = jnp.einsum(
        "ije,ek->kij", pair_out, distogram_weight, preferred_element_type=jnp.float32
    ).astype(jnp.bfloat16)
    other_bins = jnp.einsum(
        "jie,ek->kij", mirror_out, distogram_weight, preferred_element_type=jnp.float32
    ).astype(jnp.bfloat16)
    logits = (
        own_bins.astype(jnp.float32)
        + other_bins.astype(jnp.float32)
        + distogram_bias[:, None, None]
    )
    return (pair_out, logits)


def solution(mesh):
    placed = (
        P(None, ("row", "col"), None),
        P(None, ("row", "col"), None),
        P(),
        P("row", "col", None),
        P(),
        P(),
        P(),
        P(),
        P(),
        P(),
        P(),
        P(),
    )
    return jax.shard_map(
        per_device,
        mesh=mesh,
        in_specs=placed,
        out_specs=(P("row", "col", None), P(None, "row", "col")),
        check_vma=False,
    )
```

profile of v0, /device:TPU:7, one launch (start us, length us, event | category | flops | bytes accessed | tf_op | source)
XLA Modules:
  0.0 475.0 jit_solution(7178910662403680412)
XLA Ops:
  7.2 1.3 copy.53
  9.1 12.4 %all_to_all.71 = bf16[16,2,2048]{2,1,0:T(2,128)(2,1)S(1)} all-to-all(bf16[16,2,2048]{2,1,0:T(2,128)(2,1)S(1)} %reshape.64), channel_id=1, replica_groups=mesh['row'=16,'col'=2] {'row'}, dimensions={0} | all-to-all | bytes 262144 | tf_op jit(solution)/shard_map/all_to_all | solution.py:96
  22.6 5.2 %all_to_all.72 = bf16[2,2,16384]{2,1,0:T(2,128)(2,1)S(1)} all-to-all(bf16[2,2,16384]{2,1,0:T(2,128)(2,1)S(1)} %reshape.66), channel_id=1, replica_groups=mesh['row'=16,'col'=2] {'col'}, dimensions={0} | all-to-all | bytes 262144 | tf_op jit(solution)/shard_map/all_to_all | solution.py:95
  29.3 5.1 %all_gather.6 = bf16[128,32,32]{0,2,1:T(8,128)(2,1)S(1)} all-gather(bf16[128,16,32]{0,2,1:T(8,128)(2,1)S(1)} %copy-done.7), channel_id=1, replica_groups=mesh['row'=16,'col'=2] {'col'}, dimensions={1}, use_global_device_ids=true | all-gather | bytes 393216 | tf_op jit(solution)/shard_map/all_gather | solution.py:94
  34.4 35.5 %all-gather.2.cloned.1.call-done = bf16[128,256,32]{1,2,0:T(8,128)(2,1)} async-done(((bf16[8,256,32]{1,2,0:T(8,128)(2,1)}), bf16[128,256,32]{1,2,0:T(8,128)(2,1)}) %all-gather.2.cloned.1.call-update) | async-done | bytes 2097168 | tf_op jit(solution)/shard_map/all_gather | solution.py:109
  69.9 1.7 fusion.50
  71.7 1.6 copy.59
  74.4 167.7 %while.20 = (s32[]{:T(128)}, bf16[16,2,256,128]{3,2,1,0:T(8,128)(2,1)}, s32[16]{0:T(128)}, bf16[128,32,32]{0,2,1:T(8,128)(2,1)S(1)}, bf16[64,256,32]{1,0,2:T(8,1...) while((s32[]{:T(128)}, ...), condition=%wide.region_4.5_spmd, body=%wide.region_0.4_spmd.sunk | while | flops 270796800 | bytes 20274580 | solution.py:155
  74.4 1.4 dynamic_slice.49
  79.9 1.6 fusion.74
  85.0 1.3 dynamic_slice.49
  90.3 1.6 fusion.74
  100.8 1.6 fusion.74
  111.3 1.6 fusion.74
  121.7 1.6 fusion.74
  132.2 1.7 fusion.74
  142.7 1.6 fusion.74
  153.2 1.7 fusion.74
  163.6 1.6 fusion.74
  174.1 1.7 fusion.74
  184.6 1.6 fusion.74
  195.1 1.7 fusion.74
  205.5 1.6 fusion.74
  216.0 1.7 fusion.74
  226.5 1.6 fusion.74
  237.0 1.7 fusion.74
  242.1 93.0 %while.21 = (s32[]{:T(128)}, bf16[16,512,128]{2,1,0:T(8,128)(2,1)}, bf16[16,512,128]{2,1,0:T(8,128)(2,1)}, f32[128]{0:T(128)}, bf16[128,512]{1,0:T(8,128)(2,1)S(...) while((s32[]{:T(128)}, bf16[16,512,128]{2,1,0:T(8,128)(2,1)}, ...), condition=%wide.region_8.9_spmd, body=%wide.region_5.8_spmd.sunk | while | flops 204145152 | bytes 3301981 | solution.py:51
  245.6 2.4 fusion.83
  251.4 2.4 fusion.83
  257.2 2.4 fusion.83
  263.0 2.4 fusion.83
  268.8 2.4 fusion.83
  274.6 2.4 fusion.83
  280.4 2.4 fusion.83
  286.3 2.4 fusion.83
  292.1 2.4 fusion.83
  297.9 2.4 fusion.83
  303.7 2.4 fusion.83
  309.5 2.4 fusion.83
  315.3 2.4 fusion.83
  321.1 2.4 fusion.83
  326.9 2.4 fusion.83
  332.8 2.4 fusion.83
  335.1 45.3 %all_to_all.73 = bf16[32,256,128]{2,1,0:T(8,128)(2,1)S(1)} all-to-all(bf16[32,256,128]{2,1,0:T(8,128)(2,1)} %bitcast.140), channel_id=1, replica_groups=mesh['row'=16,'col'=2] {'col'}, dimensions={0} | all-to-all | bytes 4194304 | tf_op jit(solution)/shard_map/all_to_all | solution.py:60
  380.7 1.4 copy.62
  382.0 51.4 %all_to_all.74 = bf16[16,512,128]{2,0,1:T(8,128)(2,1)S(1)} all-to-all(bf16[16,512,128]{2,0,1:T(8,128)(2,1)S(1)} %copy.62), channel_id=1, replica_groups=mesh['row'=16,'col'=2] {'row'}, dimensions={1} | all-to-all | bytes 4194304 | tf_op jit(solution)/shard_map/all_to_all | solution.py:59
  434.0 28.4 %all_to_all.75 = bf16[2,8,16,32,128]{4,3,2,1,0:T(8,128)(2,1)S(1)} all-to-all(bf16[2,8,16,32,128]{4,3,2,1,0:T(8,128)(2,1)S(1)} %bitcast.145), channel_id=1, replica_groups=mesh['row'=16,'col'=2] {'col'}, dimensions={0} | all-to-all | bytes 4194304 | tf_op jit(solution)/shard_map/all_to_all | solution.py:67
  465.6 2.5 copy.66
  (482 shorter events, 183.4 us)
Async XLA Ops:
  7.2 456.1 %copy-start = (bf16[128,64]{0,1:T(8,128)(2,1)S(1)}, bf16[128,64]{0,1:T(8,128)(2,1)}, u32[]{:S(2)}) copy-start(bf16[128,64]{0,1:T(8,128)(2,1)} %param.28) | copy-start | bytes 49156
  7.2 62.8 %all-gather.2.cloned.1.call-start = ((), (), s32[]{:S(2)}) async-start(), calls=%async_computation.5 | async-start | bytes 2228224 | tf_op jit(solution)/shard_map/all_gather | solution.py:109
  21.7 7.4 %copy-start.11 = (s32[512]{0:T(512)S(1)}, s32[512]{0:T(512)}, u32[]{:S(2)}) copy-start(s32[512]{0:T(512)} %param.20) | copy-start | bytes 6148
  21.8 7.5 %copy-start.7 = (bf16[128,16,32]{0,2,1:T(8,128)(2,1)S(1)}, bf16[128,16,32]{0,2,1:T(8,128)(2,1)}, u32[]{:S(2)}) copy-start(bf16[128,16,32]{0,2,1:T(8,128)(2,1)} %param.18) | copy-start | bytes 393220
  71.7 2.7 copy-start.2
  74.4 167.7 %copy-start.3 = (bf16[128,512]{1,0:T(8,128)(2,1)S(1)}, bf16[128,512]{1,0:T(8,128)(2,1)}, u32[]{:S(2)}) copy-start(bf16[128,512]{1,0:T(8,128)(2,1)} %param.25) | copy-start | bytes 393220
  74.4 5.2 %copy-start.4 = (bf16[128,32,32]{0,2,1:T(8,128)(2,1)}, bf16[128,32,32]{0,2,1:T(8,128)(2,1)S(1)}, u32[]{:S(2)}) copy-start(bf16[128,32,32]{0,2,1:T(8,128)(2,1)S(1)} %get-tuple-element.334) | copy-start | bytes 786436 | tf_op jit(solution)/shard_map/while
  74.4 5.2 %copy-start.8 = (f32[32,256]{1,0:T(8,128)}, f32[32,256]{1,0:T(8,128)S(1)}, u32[]{:S(2)}) copy-start(f32[32,256]{1,0:T(8,128)S(1)} %get-tuple-element.336) | copy-start | bytes 98308 | tf_op jit(solution)/shard_map/while
  82.6 2.4 copy-start.5
  85.0 5.1 %copy-start.4 = (bf16[128,32,32]{0,2,1:T(8,128)(2,1)}, bf16[128,32,32]{0,2,1:T(8,128)(2,1)S(1)}, u32[]{:S(2)}) copy-start(bf16[128,32,32]{0,2,1:T(8,128)(2,1)S(1)} %get-tuple-element.334) | copy-start | bytes 786436 | tf_op jit(solution)/shard_map/while
  85.0 5.1 %copy-start.8 = (f32[32,256]{1,0:T(8,128)}, f32[32,256]{1,0:T(8,128)S(1)}, u32[]{:S(2)}) copy-start(f32[32,256]{1,0:T(8,128)S(1)} %get-tuple-element.336) | copy-start | bytes 98308 | tf_op jit(solution)/shard_map/while
  93.1 2.4 copy-start.5
  95.4 5.1 %copy-start.4 = (bf16[128,32,32]{0,2,1:T(8,128)(2,1)}, bf16[128,32,32]{0,2,1:T(8,128)(2,1)S(1)}, u32[]{:S(2)}) copy-start(bf16[128,32,32]{0,2,1:T(8,128)(2,1)S(1)} %get-tuple-element.334) | copy-start | bytes 786436 | tf_op jit(solution)/shard_map/while
  95.4 5.1 %copy-start.8 = (f32[32,256]{1,0:T(8,128)}, f32[32,256]{1,0:T(8,128)S(1)}, u32[]{:S(2)}) copy-start(f32[32,256]{1,0:T(8,128)S(1)} %get-tuple-element.336) | copy-start | bytes 98308 | tf_op jit(solution)/shard_map/while
  103.5 2.4 copy-start.5
  105.9 5.1 %copy-start.4 = (bf16[128,32,32]{0,2,1:T(8,128)(2,1)}, bf16[128,32,32]{0,2,1:T(8,128)(2,1)S(1)}, u32[]{:S(2)}) copy-start(bf16[128,32,32]{0,2,1:T(8,128)(2,1)S(1)} %get-tuple-element.334) | copy-start | bytes 786436 | tf_op jit(solution)/shard_map/while
  105.9 5.1 %copy-start.8 = (f32[32,256]{1,0:T(8,128)}, f32[32,256]{1,0:T(8,128)S(1)}, u32[]{:S(2)}) copy-start(f32[32,256]{1,0:T(8,128)S(1)} %get-tuple-element.336) | copy-start | bytes 98308 | tf_op jit(solution)/shard_map/while
  114.0 2.4 copy-start.5
  116.4 5.1 %copy-start.4 = (bf16[128,32,32]{0,2,1:T(8,128)(2,1)}, bf16[128,32,32]{0,2,1:T(8,128)(2,1)S(1)}, u32[]{:S(2)}) copy-start(bf16[128,32,32]{0,2,1:T(8,128)(2,1)S(1)} %get-tuple-element.334) | copy-start | bytes 786436 | tf_op jit(solution)/shard_map/while
  116.4 5.1 %copy-start.8 = (f32[32,256]{1,0:T(8,128)}, f32[32,256]{1,0:T(8,128)S(1)}, u32[]{:S(2)}) copy-start(f32[32,256]{1,0:T(8,128)S(1)} %get-tuple-element.336) | copy-start | bytes 98308 | tf_op jit(solution)/shard_map/while
  124.5 2.4 copy-start.5
  126.8 5.1 %copy-start.4 = (bf16[128,32,32]{0,2,1:T(8,128)(2,1)}, bf16[128,32,32]{0,2,1:T(8,128)(2,1)S(1)}, u32[]{:S(2)}) copy-start(bf16[128,32,32]{0,2,1:T(8,128)(2,1)S(1)} %get-tuple-element.334) | copy-start | bytes 786436 | tf_op jit(solution)/shard_map/while
  126.8 5.1 %copy-start.8 = (f32[32,256]{1,0:T(8,128)}, f32[32,256]{1,0:T(8,128)S(1)}, u32[]{:S(2)}) copy-start(f32[32,256]{1,0:T(8,128)S(1)} %get-tuple-element.336) | copy-start | bytes 98308 | tf_op jit(solution)/shard_map/while
  137.3 5.1 %copy-start.4 = (bf16[128,32,32]{0,2,1:T(8,128)(2,1)}, bf16[128,32,32]{0,2,1:T(8,128)(2,1)S(1)}, u32[]{:S(2)}) copy-start(bf16[128,32,32]{0,2,1:T(8,128)(2,1)S(1)} %get-tuple-element.334) | copy-start | bytes 786436 | tf_op jit(solution)/shard_map/while
  137.3 5.1 %copy-start.8 = (f32[32,256]{1,0:T(8,128)}, f32[32,256]{1,0:T(8,128)S(1)}, u32[]{:S(2)}) copy-start(f32[32,256]{1,0:T(8,128)S(1)} %get-tuple-element.336) | copy-start | bytes 98308 | tf_op jit(solution)/shard_map/while
  145.4 2.4 copy-start.5
  147.8 5.1 %copy-start.4 = (bf16[128,32,32]{0,2,1:T(8,128)(2,1)}, bf16[128,32,32]{0,2,1:T(8,128)(2,1)S(1)}, u32[]{:S(2)}) copy-start(bf16[128,32,32]{0,2,1:T(8,128)(2,1)S(1)} %get-tuple-element.334) | copy-start | bytes 786436 | tf_op jit(solution)/shard_map/while
  147.8 5.1 %copy-start.8 = (f32[32,256]{1,0:T(8,128)}, f32[32,256]{1,0:T(8,128)S(1)}, u32[]{:S(2)}) copy-start(f32[32,256]{1,0:T(8,128)S(1)} %get-tuple-element.336) | copy-start | bytes 98308 | tf_op jit(solution)/shard_map/while
  158.3 5.1 %copy-start.4 = (bf16[128,32,32]{0,2,1:T(8,128)(2,1)}, bf16[128,32,32]{0,2,1:T(8,128)(2,1)S(1)}, u32[]{:S(2)}) copy-start(bf16[128,32,32]{0,2,1:T(8,128)(2,1)S(1)} %get-tuple-element.334) | copy-start | bytes 786436 | tf_op jit(solution)/shard_map/while
  158.3 5.1 %copy-start.8 = (f32[32,256]{1,0:T(8,128)}, f32[32,256]{1,0:T(8,128)S(1)}, u32[]{:S(2)}) copy-start(f32[32,256]{1,0:T(8,128)S(1)} %get-tuple-element.336) | copy-start | bytes 98308 | tf_op jit(solution)/shard_map/while
  166.4 2.4 copy-start.5
  168.7 5.1 %copy-start.4 = (bf16[128,32,32]{0,2,1:T(8,128)(2,1)}, bf16[128,32,32]{0,2,1:T(8,128)(2,1)S(1)}, u32[]{:S(2)}) copy-start(bf16[128,32,32]{0,2,1:T(8,128)(2,1)S(1)} %get-tuple-element.334) | copy-start | bytes 786436 | tf_op jit(solution)/shard_map/while
  168.8 5.1 %copy-start.8 = (f32[32,256]{1,0:T(8,128)}, f32[32,256]{1,0:T(8,128)S(1)}, u32[]{:S(2)}) copy-start(f32[32,256]{1,0:T(8,128)S(1)} %get-tuple-element.336) | copy-start | bytes 98308 | tf_op jit(solution)/shard_map/while
  179.2 5.1 %copy-start.4 = (bf16[128,32,32]{0,2,1:T(8,128)(2,1)}, bf16[128,32,32]{0,2,1:T(8,128)(2,1)S(1)}, u32[]{:S(2)}) copy-start(bf16[128,32,32]{0,2,1:T(8,128)(2,1)S(1)} %get-tuple-element.334) | copy-start | bytes 786436 | tf_op jit(solution)/shard_map/while
  179.2 5.1 %copy-start.8 = (f32[32,256]{1,0:T(8,128)}, f32[32,256]{1,0:T(8,128)S(1)}, u32[]{:S(2)}) copy-start(f32[32,256]{1,0:T(8,128)S(1)} %get-tuple-element.336) | copy-start | bytes 98308 | tf_op jit(solution)/shard_map/while
  187.3 2.4 copy-start.5
  189.7 5.1 %copy-start.4 = (bf16[128,32,32]{0,2,1:T(8,128)(2,1)}, bf16[128,32,32]{0,2,1:T(8,128)(2,1)S(1)}, u32[]{:S(2)}) copy-start(bf16[128,32,32]{0,2,1:T(8,128)(2,1)S(1)} %get-tuple-element.334) | copy-start | bytes 786436 | tf_op jit(solution)/shard_map/while
  189.7 5.1 %copy-start.8 = (f32[32,256]{1,0:T(8,128)}, f32[32,256]{1,0:T(8,128)S(1)}, u32[]{:S(2)}) copy-start(f32[32,256]{1,0:T(8,128)S(1)} %get-tuple-element.336) | copy-start | bytes 98308 | tf_op jit(solution)/shard_map/while
  200.2 5.1 %copy-start.4 = (bf16[128,32,32]{0,2,1:T(8,128)(2,1)}, bf16[128,32,32]{0,2,1:T(8,128)(2,1)S(1)}, u32[]{:S(2)}) copy-start(bf16[128,32,32]{0,2,1:T(8,128)(2,1)S(1)} %get-tuple-element.334) | copy-start | bytes 786436 | tf_op jit(solution)/shard_map/while
  200.2 5.1 %copy-start.8 = (f32[32,256]{1,0:T(8,128)}, f32[32,256]{1,0:T(8,128)S(1)}, u32[]{:S(2)}) copy-start(f32[32,256]{1,0:T(8,128)S(1)} %get-tuple-element.336) | copy-start | bytes 98308 | tf_op jit(solution)/shard_map/while
  208.3 2.4 copy-start.5
  210.7 5.1 %copy-start.4 = (bf16[128,32,32]{0,2,1:T(8,128)(2,1)}, bf16[128,32,32]{0,2,1:T(8,128)(2,1)S(1)}, u32[]{:S(2)}) copy-start(bf16[128,32,32]{0,2,1:T(8,128)(2,1)S(1)} %get-tuple-element.334) | copy-start | bytes 786436 | tf_op jit(solution)/shard_map/while
  210.7 5.1 %copy-start.8 = (f32[32,256]{1,0:T(8,128)}, f32[32,256]{1,0:T(8,128)S(1)}, u32[]{:S(2)}) copy-start(f32[32,256]{1,0:T(8,128)S(1)} %get-tuple-element.336) | copy-start | bytes 98308 | tf_op jit(solution)/shard_map/while
  221.1 5.1 %copy-start.4 = (bf16[128,32,32]{0,2,1:T(8,128)(2,1)}, bf16[128,32,32]{0,2,1:T(8,128)(2,1)S(1)}, u32[]{:S(2)}) copy-start(bf16[128,32,32]{0,2,1:T(8,128)(2,1)S(1)} %get-tuple-element.334) | copy-start | bytes 786436 | tf_op jit(solution)/shard_map/while
  221.1 5.1 %copy-start.8 = (f32[32,256]{1,0:T(8,128)}, f32[32,256]{1,0:T(8,128)S(1)}, u32[]{:S(2)}) copy-start(f32[32,256]{1,0:T(8,128)S(1)} %get-tuple-element.336) | copy-start | bytes 98308 | tf_op jit(solution)/shard_map/while
  229.2 2.4 copy-start.5
  231.6 5.1 %copy-start.4 = (bf16[128,32,32]{0,2,1:T(8,128)(2,1)}, bf16[128,32,32]{0,2,1:T(8,128)(2,1)S(1)}, u32[]{:S(2)}) copy-start(bf16[128,32,32]{0,2,1:T(8,128)(2,1)S(1)} %get-tuple-element.334) | copy-start | bytes 786436 | tf_op jit(solution)/shard_map/while
  231.6 5.1 %copy-start.8 = (f32[32,256]{1,0:T(8,128)}, f32[32,256]{1,0:T(8,128)S(1)}, u32[]{:S(2)}) copy-start(f32[32,256]{1,0:T(8,128)S(1)} %get-tuple-element.336) | copy-start | bytes 98308 | tf_op jit(solution)/shard_map/while
  (56 other events, 100.5 us)
Sparse Core Ops, SparseCore 0:
  29.2 40.6 all-gather.1
where the time goes:
time: 481 us; the launch traced here: 475 us
  blocking collectives  148 us (31%)
  local copies, waits for them, and re-layouts  105 us (22%)
  matrix products  93.8 us (20%)
  other arithmetic  55.6 us (12%)
  waiting for transfers between devices  35.5 us (7%)
  loops' own time  23 us (5%)
  between operations  14.2 us (3%)
    all_to_all x1, blocking collectives, mirror_tile(): lax.all_to_all(lax.all_to_all(pair_tile, 'col', split_axis=0, concat_axis...  51.4 us
    all_to_all x1, blocking collectives, mirror_tile(): lax.all_to_all(pair_tile, 'col', split_axis=0, concat_axis=1, tiled=True)  45.3 us
    dot_general x16, matrix products, transition_rows(): jnp.dot(hidden, transition_down_weight, preferred_element_type=jnp.float32)  37.7 us
    all_gather x1, waiting for transfers between devices, per_device(): right_cols = lax.all_gather(relaid, 'row', axis=0, tiled=True)  35.5 us
    all_to_all x1, blocking collectives, mirror_tile(): lax.all_to_all(regrouped, 'col', split_axis=0, concat_axis=2, tiled=True)  28.4 us
    dot_general x16, matrix products, outer_block(): jnp.einsum('sic,sjd->ijcd', left_block[:alignment_slab_length], paired_ri...  26.4 us
    another operation x1, loops' own time, per_device(): lax.map(outer_block, jnp.arange(block_count, dtype=jnp.int32))  22.5 us
    dynamic_slice x16, local copies, waits for them, and re-layouts, per_device(): lax.map(outer_block, jnp.arange(block_count, dtype=jnp.int32))  20.6 us
  transfers between devices with their start and end apart: 1, of which 1 were waited for; matrix products, arithmetic and copies ran while one was open for 0% of the time, Pallas kernels for 0%

commit v1 on v0

v1 whole, which is shorter than its diff:
```python
import functools

import jax
import jax.numpy as jnp
from jax import lax
from jax.experimental import pallas as pl
from jax.experimental.pallas import tpu as pltpu
from jax.sharding import PartitionSpec as P

MESH = pl.DeviceIdType.MESH
VMEM_BYTES = 56 * 1024 * 1024


def pair_kernel(
    slab,
    width,
    group,
    rows_tile,
    chain_rows,
    chain_cols,
    left,
    right,
    incoming,
    mixing,
    bias,
    gain,
    gate_up,
    down,
    bins_weight,
    pair_out,
    own_bins,
    turned_bins,
    lhs,
    weights,
    outer,
    bins,
):
    step = pl.program_id(0)
    cols_tile = right.shape[1]
    sequences = 2 * slab
    channels = mixing.shape[0]
    hid = down.shape[1]
    bins_count = bins_weight.shape[0]
    sides, _, lanes = bins.shape
    first_row = step * group
    first_chain = chain_rows[first_row]
    last_chain = chain_rows[first_row + group - 1]

    def load_chains(low):
        lane = lax.broadcasted_iota(jnp.int32, (cols_tile, sequences), 1)
        apart = jnp.where(lane < slab, 1.0 / slab, 0.0).astype(jnp.float32)
        for half in range(2):
            chain = low + half
            same = chain_cols[...] == chain
            weights[:, half * sequences : (half + 1) * sequences] = jnp.where(
                same, 0.5 / slab, apart
            ).astype(jnp.bfloat16)
            for row in range(group):
                keep = jnp.where(chain_rows[first_row + row] == chain, 1.0, 0.0)
                lhs[row * width : (row + 1) * width, half * sequences : (half + 1) * sequences] = (
                    left[row * width : (row + 1) * width, :].astype(jnp.float32) * keep
                ).astype(jnp.bfloat16)

    def outer_part(depth):
        block = right[depth]
        spread = jnp.concatenate([block, block], axis=1) * weights[...]
        part = lax.dot_general(
            lhs[...], spread, (((1,), (1,)), ((), ())), preferred_element_type=jnp.float32
        )
        return part.astype(jnp.bfloat16).reshape(group, width, cols_tile)

    def place(depth):
        return pl.ds(pl.multiple_of(depth * width, width), width)

    load_chains(first_chain)

    @pl.loop(0, width, unroll=4)
    def _(depth):
        outer[:, place(depth), :] = outer_part(depth)

    @pl.loop(1, (last_chain - first_chain) // 2 + 1)
    def _(turn):
        load_chains(first_chain + 2 * turn)

        @pl.loop(0, width)
        def _(depth):
            outer[:, place(depth), :] = outer[:, place(depth), :] + outer_part(depth)

    def one_row(row):
        mid = jnp.dot(mixing[...], outer[row], preferred_element_type=jnp.float32)
        mid = mid + bias[...] + incoming[row].astype(jnp.float32).T
        mid = mid.astype(jnp.bfloat16).astype(jnp.float32)
        center = jnp.mean(mid, axis=0, keepdims=True)
        shifted = mid - center
        spread = jnp.mean(shifted * shifted, axis=0, keepdims=True)
        normed = (shifted * lax.rsqrt(spread + 1e-05) * gain[...]).astype(jnp.bfloat16)
        both = jnp.dot(gate_up[...], normed, preferred_element_type=jnp.float32)
        half_gate = 0.5 * both[:hid]
        hidden = ((half_gate + half_gate * jnp.tanh(half_gate)) * both[hid:]).astype(jnp.bfloat16)
        result = mid + jnp.dot(down[...], hidden, preferred_element_type=jnp.float32)
        rounded = result.astype(jnp.bfloat16)
        pair_out[row] = result.T.astype(jnp.bfloat16)
        projected = jnp.dot(bins_weight[...], rounded, preferred_element_type=jnp.float32)
        for side in range(sides):
            bins[side, pl.ds(first_row + row, bins_count, stride=rows_tile), :] = projected[
                :, side * lanes : (side + 1) * lanes
            ]

    @pl.loop(0, group // 2)
    def _(pair):
        for half in range(2):
            one_row(2 * pair + half)

    @pl.when(step == pl.num_programs(0) - 1)
    def _():
        for side in range(sides):
            columns = slice(side * lanes, (side + 1) * lanes)
            own_bins[:, :, columns] = (
                bins[side].astype(jnp.bfloat16).reshape(bins_count, rows_tile, lanes)
            )
            for part in range(turned_bins.shape[0]):
                turned_bins[part, columns, :] = bins[
                    side, part * lanes : (part + 1) * lanes, :
                ].T.astype(jnp.bfloat16)


def exchange_kernel(
    row_groups, rows_tile, turned_bins, own_bins, bias, logits, landed, send_sem, recv_sem, own_sem
):
    row_at = lax.axis_index("row")
    col_at = lax.axis_index("col")
    mine = lax.rem(row_at, row_groups)
    peer_col = row_at // row_groups
    inside = peer_col == col_at

    def remote(slot):
        return jnp.logical_or(jnp.logical_not(inside), slot != mine)

    def peer(slot):
        return (col_at * row_groups + slot, peer_col)

    def block(slot):
        return turned_bins.at[:, pl.ds(pl.multiple_of(slot * rows_tile, rows_tile), rows_tile), :]

    def copy(slot):
        return pltpu.make_async_remote_copy(
            src_ref=block(slot),
            dst_ref=landed.at[mine],
            send_sem=send_sem.at[slot],
            recv_sem=recv_sem.at[mine],
            device_id=peer(slot),
            device_id_type=MESH,
        )

    def arrival(slot):
        return pltpu.make_async_remote_copy(
            src_ref=block(slot),
            dst_ref=landed.at[slot],
            send_sem=send_sem.at[slot],
            recv_sem=recv_sem.at[slot],
            device_id=peer(slot),
            device_id_type=MESH,
        )

    barrier = pltpu.get_barrier_semaphore()
    for slot in range(row_groups):

        @pl.when(remote(slot))
        def _():
            pl.semaphore_signal(barrier, inc=1, device_id=peer(slot), device_id_type=MESH)

    pl.semaphore_wait(barrier, jnp.where(inside, row_groups - 1, row_groups))

    for turn in range(row_groups):
        slot = lax.rem(mine + turn, row_groups)

        @pl.when(remote(slot))
        def _():
            copy(slot).start()

    @pl.when(inside)
    def _():
        local = pltpu.make_async_copy(block(mine), landed.at[mine], own_sem)
        local.start()
        local.wait()

    for turn in range(row_groups):
        slot = lax.rem(mine + turn, row_groups)

        @pl.when(remote(slot))
        def _():
            arrival(slot).wait_recv()
            copy(slot).wait_send()

    parts, lanes = landed.shape[1], landed.shape[3]
    each = lanes // rows_tile

    @pl.loop(0, parts)
    def _(part):
        got = [landed[slot, part].astype(jnp.float32) for slot in range(row_groups)]
        for inner in range(each):
            mirrored = jnp.concatenate(
                [one[:, inner * rows_tile : (inner + 1) * rows_tile] for one in got], axis=1
            )
            at = part * each + inner
            logits[at] = own_bins[at].astype(jnp.float32) + mirrored + bias[at]


def per_device(
    first_homolog_embedding,
    second_homolog_embedding,
    token_chain_index,
    incoming_pair_state,
    tensor_mixing_matrix,
    outer_product_bias,
    transition_norm_gain,
    transition_gate_weight,
    transition_up_weight,
    transition_down_weight,
    distogram_weight,
    distogram_bias,
):
    row_count = lax.axis_size("row")
    col_count = lax.axis_size("col")
    row_at = lax.axis_index("row")
    col_at = lax.axis_index("col")
    rows_tile, cols_tile, channels = incoming_pair_state.shape
    sequences, tokens_local, width = first_homolog_embedding.shape
    hid = transition_gate_weight.shape[1]
    bins_count = distogram_weight.shape[1]
    row_groups = row_count // col_count
    slab = sequences // 2
    f32, bf16 = jnp.float32, jnp.bfloat16

    left = lax.all_gather(
        jnp.transpose(first_homolog_embedding, (1, 2, 0)), "col", axis=0, tiled=True
    ).reshape(rows_tile * width, sequences)
    right = lax.all_gather(
        jnp.transpose(second_homolog_embedding, (1, 2, 0)), ("row", "col"), axis=0, tiled=True
    )
    right = lax.dynamic_slice_in_dim(right, col_at * cols_tile, cols_tile, 0)
    right = jnp.transpose(right, (1, 0, 2))

    chain_rows = lax.dynamic_slice_in_dim(token_chain_index, row_at * rows_tile, rows_tile, 0)
    chain_cols = lax.dynamic_slice_in_dim(token_chain_index, col_at * cols_tile, cols_tile, 0)
    chain_cols = jnp.broadcast_to(chain_cols[:, None], (cols_tile, sequences))
    mixing = jnp.transpose(
        tensor_mixing_matrix.reshape(width, width, channels), (2, 1, 0)
    ).reshape(channels, width * width)
    bias = jnp.broadcast_to(outer_product_bias[:, None], (channels, cols_tile))
    gain = jnp.broadcast_to(transition_norm_gain[:, None], (channels, cols_tile))
    gate_up = jnp.concatenate([transition_gate_weight.T, transition_up_weight.T], axis=0)

    group = min(16, rows_tile)
    lanes = 128
    parts = bins_count * rows_tile // lanes

    def whole(*shape):
        return pl.BlockSpec(shape, lambda step: (0,) * len(shape))

    pair_out, own_bins, turned_bins = pl.pallas_call(
        functools.partial(pair_kernel, slab, width, group, rows_tile),
        grid=(rows_tile // group,),
        in_specs=[
            pl.BlockSpec(memory_space=pltpu.SMEM),
            whole(cols_tile, sequences),
            pl.BlockSpec((group * width, sequences), lambda step: (step, 0)),
            whole(width, cols_tile, sequences),
            pl.BlockSpec((group, cols_tile, channels), lambda step: (step, 0, 0)),
            whole(channels, width * width),
            whole(channels, cols_tile),
            whole(channels, cols_tile),
            whole(2 * hid, channels),
            whole(channels, hid),
            whole(bins_count, channels),
        ],
        out_specs=[
            pl.BlockSpec((group, cols_tile, channels), lambda step: (step, 0, 0)),
            whole(bins_count, rows_tile, cols_tile),
            whole(parts, cols_tile, lanes),
        ],
        out_shape=[
            jax.ShapeDtypeStruct((rows_tile, cols_tile, channels), bf16),
            jax.ShapeDtypeStruct((bins_count, rows_tile, cols_tile), bf16),
            jax.ShapeDtypeStruct((parts, cols_tile, lanes), bf16),
        ],
        scratch_shapes=[
            pltpu.VMEM((group * width, 2 * sequences), bf16),
            pltpu.VMEM((cols_tile, 2 * sequences), bf16),
            pltpu.VMEM((group, width * width, cols_tile), bf16),
            pltpu.VMEM((cols_tile // lanes, bins_count * rows_tile, lanes), f32),
        ],
        compiler_params=pltpu.CompilerParams(vmem_limit_bytes=VMEM_BYTES),
        name="pair_tile",
    )(
        chain_rows,
        chain_cols,
        left,
        right,
        incoming_pair_state,
        mixing,
        bias,
        gain,
        gate_up,
        transition_down_weight.T,
        distogram_weight.T,
    )

    vmem = pl.BlockSpec(memory_space=pltpu.VMEM)
    logits = pl.pallas_call(
        functools.partial(exchange_kernel, row_groups, rows_tile),
        in_specs=[vmem, vmem, pl.BlockSpec(memory_space=pltpu.SMEM)],
        out_specs=vmem,
        out_shape=jax.ShapeDtypeStruct((bins_count, rows_tile, cols_tile), f32),
        scratch_shapes=[
            pltpu.VMEM((row_groups, parts, rows_tile, lanes), bf16),
            pltpu.SemaphoreType.DMA((row_groups,)),
            pltpu.SemaphoreType.DMA((row_groups,)),
            pltpu.SemaphoreType.DMA,
        ],
        compiler_params=pltpu.CompilerParams(
            collective_id=0, has_side_effects=True, vmem_limit_bytes=VMEM_BYTES
        ),
        name="mirror_bins",
    )(turned_bins, own_bins, distogram_bias)
    return (pair_out, logits)


def solution(mesh):
    placed = (
        P(None, ("row", "col"), None),
        P(None, ("row", "col"), None),
        P(),
        P("row", "col", None),
        P(),
        P(),
        P(),
        P(),
        P(),
        P(),
        P(),
        P(),
    )
    return jax.shard_map(
        per_device,
        mesh=mesh,
        in_specs=placed,
        out_specs=(P("row", "col", None), P(None, "row", "col")),
        check_vma=False,
    )
```

time: 481 us -> 198 us (0.41)
  the two profiles are of different devices: /device:TPU:7 before, /device:TPU:19 now
where the time goes in v1:
time: 198 us; the launch traced here: 201 us
  Pallas kernels  108 us (55%)
  waiting for transfers between devices  55.2 us (28%)
  local copies, waits for them, and re-layouts  17.8 us (9%)
  between operations  14.1 us (7%)
  blocking collectives  5.14 us (3%)
    pallas_call x1, Pallas kernels, per_device(): pl.pallas_call(functools.partial(exchange_kernel, row_groups, rows_tile),...  63.4 us
    all_gather x1, waiting for transfers between devices, per_device(): lax.all_gather(jnp.transpose(second_homolog_embedding, (1, 2, 0)), ('row'...  55.1 us
    pallas_call x1, Pallas kernels, per_device(): pl.pallas_call(functools.partial(pair_kernel, slab, width, group, rows_ti...  44.2 us
    unnamed x11, local copies, waits for them, and re-layouts  8.53 us
    all_gather x1, blocking collectives, per_device(): lax.all_gather(jnp.transpose(first_homolog_embedding, (1, 2, 0)), 'col',...  5.14 us
  transfers between devices with their start and end apart: 1, of which 1 were waited for; matrix products, arithmetic and copies ran while one was open for 4% of the time, Pallas kernels for 0%

profile of v1, /device:TPU:19, one launch (start us, length us, event | category | flops | bytes accessed | tf_op | source)
XLA Modules:
  0.0 200.6 jit_solution(10964519053071798423)
XLA Ops:
  7.2 0.0 copy-start
  7.2 0.0 all-gather.2.cloned.1.call-start
  7.2 1.6 copy.37
  8.9 0.0 all-gather.2.cloned.1.call-update
  8.9 1.3 dynamic_slice.9.chain_rows
  10.2 0.8 dynamic_slice.10
  10.9 1.0 copy.32
  12.0 1.0 copy.33
  13.0 1.7 copy.34
  14.7 1.1 copy.31
  15.7 0.9 copy.35.mixing
  16.6 0.0 copy-done
  16.6 5.1 %all_gather.6 = bf16[32,32,128]{2,1,0:T(8,128)(2,1)} all-gather(bf16[16,32,128]{2,1,0:T(8,128)(2,1)S(1)} %bitcast.22), channel_id=1, replica_groups=mesh['row'=16,'col'=2] {'col'}, dimensions={0}, use_global_device_ids=true | all-gather | bytes 393216 | tf_op jit(solution)/shard_map/all_gather | solution.py:235
  21.7 0.7 pad_maximum_fusion.gate_up
  22.5 0.0 copy-start.1
  22.5 0.0 copy-start.2
  22.5 55.1 %all-gather.2.cloned.1.call-done = bf16[512,32,128]{2,0,1:T(8,128)(2,1)} async-done(((bf16[16,32,128]{2,0,1:T(8,128)(2,1)}), bf16[512,32,128]{2,0,1:T(8,128)(2,1)}) %all-gather.2.cloned.1.call-update) | async-done | bytes 4194320 | tf_op jit(solution)/shard_map/all_gather | solution.py:238
  77.6 3.1 %dynamic-slice_bitcast_fusion.right = bf16[32,256,128]{2,1,0:T(8,128)(2,1)} fusion(bf16[512,32,128]{2,0,1:T(8,128)(2,1)} %all-gather.2.cloned.1.call-done, s32[]{:T(128)S(6)} %select_n.8), kind=kLoop, calls=%fused_computation | loop fusion | bytes 4194308 | tf_op jit(solution)/shard_map/transpose | solution.py:242
  80.8 0.7 broadcast_in_dim.6.chain_cols
  81.5 0.0 copy-done.1
  81.5 0.7 broadcast_in_dim.7.bias
  82.2 0.0 copy-done.2
  82.2 0.7 broadcast_in_dim.8.gain
  83.0 44.2 %pair_tile.1 = (bf16[32,256,128]{2,1,0:T(8,128)(2,1)}, bf16[64,32,256]{2,1,0:T(8,128)(2,1)}, bf16[16,256,128]{2,1,0:T(8,128)(2,1)}) custom-call(s32[32]{0:T(128)} %dynamic_slice.9.chain_rows, s32[256,128]{1,0:T(8,128)} %broadcast_in_dim.6.chain_cols, bf16[1024,128]{1,0:T(8,128)(2,1)} %bitcast.15, bf16[32,256,128]{2,1,0:T(8,128)(2,1)} %dynamic-slice_bitcast_fusion.right, ...), custom_call_target="tpu_custom_call" | custom-call | tf_op jit(solution)/shard_map/pair_tile/pallas_call | solution.py:261
  127.2 63.4 %mirror_bins.1 = f32[64,32,256]{2,1,0:T(8,128)} custom-call(bf16[16,256,128]{2,1,0:T(8,128)(2,1)} %get-tuple-element.6.turned_bins, bf16[64,32,256]{2,1,0:T(8,128)(2,1)} %get-tuple-element.7.own_bins, f32[64]{0:T(128)} %bias.1), custom_call_target="tpu_custom_call" | custom-call | tf_op jit(solution)/shard_map/mirror_bins/pallas_call | solution.py:310
  190.6 3.2 %copy.39 = f32[64,32,256]{2,1,0:T(8,128)} copy(f32[64,32,256]{2,1,0:T(8,128)} %mirror_bins.1) | data formatting | bytes 4194304
Async XLA Ops:
  7.2 9.4 %copy-start = (bf16[128,16,32]{0,2,1:T(8,128)(2,1)S(1)}, bf16[128,16,32]{0,2,1:T(8,128)(2,1)}, u32[]{:S(2)}) copy-start(bf16[128,16,32]{0,2,1:T(8,128)(2,1)} %param.12) | copy-start | bytes 393220
  7.2 70.5 %all-gather.2.cloned.1.call-start = ((), (), s32[]{:S(2)}) async-start(), calls=%async_computation | async-start | bytes 4325376 | tf_op jit(solution)/shard_map/all_gather | solution.py:238
  22.5 59.0 %copy-start.1 = (f32[128]{0:T(128)S(1)}, f32[128]{0:T(128)}, u32[]{:S(2)}) copy-start(f32[128]{0:T(128)} %param.17) | copy-start | bytes 1540
  22.5 59.8 %copy-start.2 = (f32[128]{0:T(128)S(1)}, f32[128]{0:T(128)}, u32[]{:S(2)}) copy-start(f32[128]{0:T(128)} %param.18) | copy-start | bytes 1540
Sparse Core Ops, SparseCore 0:
  11.5 66.1 all-gather.1

commit v2 on v1

--- a/solution.py
+++ b/solution.py
@@ -36,7 +36,7 @@
     bins,
 ):
     step = pl.program_id(0)
-    cols_tile = right.shape[1]
+    cols_tile = chain_cols.shape[0]
     sequences = 2 * slab
     channels = mixing.shape[0]
     hid = down.shape[1]
@@ -62,7 +62,9 @@
                 ).astype(jnp.bfloat16)
 
     def outer_part(depth):
-        block = right[depth]
+        tokens = right.shape[1] // width
+        block = right[:, pl.ds(pl.multiple_of(depth * tokens, tokens), tokens), :]
+        block = block.reshape(cols_tile, sequences)
         spread = jnp.concatenate([block, block], axis=1) * weights[...]
         part = lax.dot_general(
             lhs[...], spread, (((1,), (1,)), ((), ())), preferred_element_type=jnp.float32
@@ -74,7 +76,7 @@
 
     load_chains(first_chain)
 
-    @pl.loop(0, width, unroll=4)
+    @pl.loop(0, width, unroll=8)
     def _(depth):
         outer[:, place(depth), :] = outer_part(depth)
 
@@ -106,10 +108,10 @@
                 :, side * lanes : (side + 1) * lanes
             ]
 
-    @pl.loop(0, group // 2)
-    def _(pair):
-        for half in range(2):
-            one_row(2 * pair + half)
+    @pl.loop(0, group // 4)
+    def _(quad):
+        for part in range(4):
+            one_row(4 * quad + part)
 
     @pl.when(step == pl.num_programs(0) - 1)
     def _():
@@ -124,73 +126,352 @@
                 ].T.astype(jnp.bfloat16)
 
 
-def exchange_kernel(
-    row_groups, rows_tile, turned_bins, own_bins, bias, logits, landed, send_sem, recv_sem, own_sem
+def gather_kernel(
+    row_groups,
+    col_count,
+    first,
+    second,
+    left,
+    right,
+    crossed,
+    left_send,
+    left_recv,
+    cross_send,
+    cross_recv,
+    swap_send,
+    swap_recv,
+    group_send,
+    group_recv,
+    core_send,
+    core_recv,
+    own_sem,
 ):
     row_at = lax.axis_index("row")
-    col_at = lax.axis_index("col")
-    mine = lax.rem(row_at, row_groups)
-    peer_col = row_at // row_groups
-    inside = peer_col == col_at
-
-    def remote(slot):
-        return jnp.logical_or(jnp.logical_not(inside), slot != mine)
-
-    def peer(slot):
-        return (col_at * row_groups + slot, peer_col)
+    col = lax.axis_index("col")
+    group = row_at // row_groups
+    place = lax.rem(row_at, row_groups)
+    partner = place + 1 - 2 * lax.rem(place, 2)
+
+    def device(to_group, to_place, to_col):
+        return (to_group * row_groups + to_place, to_col)
+
+    def other(step, at):
+        return lax.rem(at + step, col_count)
+
+    def in_group(step):
+        return lax.rem(place + 2 * step, row_groups)
+
+    def remote(src, dst, send, recv, target):
+        return pltpu.make_async_remote_copy(
+            src_ref=src,
+            dst_ref=dst,
+            send_sem=send,
+            recv_sem=recv,
+            device_id=target,
+            device_id_type=MESH,
+        )
+
+    def run(at):
+        return right.at[pl.ds(at * col_count, col_count)]
+
+    across = range(1, col_count)
+    around = range(1, row_groups // 2)
+    barrier = pltpu.get_barrier_semaphore()
+    for step in across:
+        for target in (device(other(step, group), place, col), device(group, place, other(step, col))):
+            pl.semaphore_signal(barrier, inc=1, device_id=target, device_id_type=MESH)
+    for step in around:
+        pl.semaphore_signal(
+            barrier, inc=1, device_id=device(group, in_group(step), col), device_id_type=MESH
+        )
+    pl.semaphore_signal(
+        barrier, inc=1, device_id=device(group, partner, col), device_id_type=MESH
+    )
+    pl.semaphore_wait(barrier, 2 * (col_count - 1) + row_groups // 2)
+
+    def cross(step):
+        to = other(step, group)
+        return remote(
+            second, crossed.at[group], cross_send.at[to], cross_recv.at[group], device(to, place, col)
+        )
+
+    def crossing(source):
+        return remote(
+            second,
+            crossed.at[source],
+            cross_send.at[source],
+            cross_recv.at[source],
+            device(source, place, col),
+        )
+
+    def left_copy(step, at):
+        to = other(step, col)
+        return remote(
+            first, left.at[at], left_send.at[to], left_recv.at[at], device(group, place, to)
+        )
+
+    def swap(step, at):
+        to = other(step, col)
+        return remote(
+            crossed.at[to],
+            right.at[place * col_count + at],
+            swap_send.at[to],
+            swap_recv.at[at],
+            device(group, place, to),
+        )
+
+    def share(step, at):
+        to = in_group(step)
+        return remote(
+            run(at), run(at), group_send.at[to], group_recv.at[at], device(group, to, col)
+        )
+
+    def hand(mine, theirs):
+        return remote(
+            run(mine),
+            run(theirs),
+            core_send.at[mine],
+            core_recv.at[theirs],
+            device(group, partner, col),
+        )
+
+    for step in across:
+        cross(step).start()
+    own = pltpu.make_async_copy(second, crossed.at[group], own_sem.at[0])
+    own.start()
+    own_left = pltpu.make_async_copy(first, left.at[col], own_sem.at[1])
+    own_left.start()
+    own.wait()
+    own_left.wait()
+    for step in across:
+        left_copy(step, col).start()
+
+    for step in range(col_count):
+        wanted = other(step, group)
+        if step:
+            crossing(wanted).wait_recv()
+
+        @pl.when(wanted != col)
+        def _():
+            remote(
+                crossed.at[wanted],
+                right.at[place * col_count + col],
+                swap_send.at[wanted],
+                swap_recv.at[col],
+                device(group, place, wanted),
+            ).start()
+
+        @pl.when(wanted == col)
+        def _():
+            kept = pltpu.make_async_copy(
+                crossed.at[wanted], right.at[place * col_count + col], own_sem.at[2]
+            )
+            kept.start()
+            kept.wait()
+
+    for step in across:
+        swap(step, other(step, col)).wait_recv()
+    for step in around:
+        share(step, place).start()
+    hand(place, place).start()
+    for step in around:
+        share(step, in_group(step)).wait_recv()
+        hand(in_group(step), in_group(step)).start()
+    for step in range(row_groups // 2):
+        theirs = lax.rem(partner + 2 * step, row_groups)
+        mine = in_group(step)
+        hand(mine, theirs).wait_recv()
+    for step in range(row_groups // 2):
+        hand(in_group(step), in_group(step)).wait_send()
+    for step in around:
+        share(step, place).wait_send()
+    for step in across:
+        left_copy(step, other(step, col)).wait_recv()
+        left_copy(step, col).wait_send()
+        swap(step, col).wait_send()
+        cross(step).wait_send()
+
+
+def exchange_kernel(
+    row_groups,
+    col_count,
+    rows_tile,
+    turned_bins,
+    own_bins,
+    bias,
+    logits,
+    landed,
+    group_relay,
+    col_relay,
+    send_sem,
+    recv_sem,
+    group_recv,
+    col_recv,
+    group_send,
+    col_send,
+    own_sem,
+):
+    row_at = lax.axis_index("row")
+    col = lax.axis_index("col")
+    group = row_at // row_groups
+    place = lax.rem(row_at, row_groups)
+    inside = group == col
+    half = row_groups // 2
+    lower = place < half
+
+    def device(to_group, to_place, to_col):
+        return (to_group * row_groups + to_place, to_col)
+
+    def remote(src, dst, send, recv, target):
+        return pltpu.make_async_remote_copy(
+            src_ref=src,
+            dst_ref=dst,
+            send_sem=send,
+            recv_sem=recv,
+            device_id=target,
+            device_id_type=MESH,
+        )
 
     def block(slot):
         return turned_bins.at[:, pl.ds(pl.multiple_of(slot * rows_tile, rows_tile), rows_tile), :]
 
-    def copy(slot):
-        return pltpu.make_async_remote_copy(
-            src_ref=block(slot),
-            dst_ref=landed.at[mine],
-            send_sem=send_sem.at[slot],
-            recv_sem=recv_sem.at[mine],
-            device_id=peer(slot),
-            device_id_type=MESH,
-        )
-
-    def arrival(slot):
-        return pltpu.make_async_remote_copy(
-            src_ref=block(slot),
-            dst_ref=landed.at[slot],
-            send_sem=send_sem.at[slot],
-            recv_sem=recv_sem.at[slot],
-            device_id=peer(slot),
-            device_id_type=MESH,
-        )
-
     barrier = pltpu.get_barrier_semaphore()
-    for slot in range(row_groups):
-
-        @pl.when(remote(slot))
-        def _():
-            pl.semaphore_signal(barrier, inc=1, device_id=peer(slot), device_id_type=MESH)
-
-    pl.semaphore_wait(barrier, jnp.where(inside, row_groups - 1, row_groups))
-
-    for turn in range(row_groups):
-        slot = lax.rem(mine + turn, row_groups)
-
-        @pl.when(remote(slot))
-        def _():
-            copy(slot).start()
+
+    def greet(target):
+        pl.semaphore_signal(barrier, inc=1, device_id=target, device_id_type=MESH)
+
+    def others():
+        return [lax.rem(col + step, col_count) for step in range(1, col_count)]
+
+    def near_slot(step):
+        return lax.rem(place + step, row_groups)
 
     @pl.when(inside)
     def _():
-        local = pltpu.make_async_copy(block(mine), landed.at[mine], own_sem)
+        for step in range(1, row_groups):
+            greet(device(group, near_slot(step), col))
+        for other in others():
+            for index in range(half):
+                greet(device(group, index, other))
+                greet(device(other, half + index, col))
+
+            @pl.when(lower)
+            def _():
+                greet(device(other, place, col))
+
+            @pl.when(jnp.logical_not(lower))
+            def _():
+                greet(device(group, place, other))
+
+    @pl.when(jnp.logical_not(inside))
+    def _():
+        @pl.when(lower)
+        def _():
+            for slot in range(row_groups):
+                greet(device(group, slot, group))
+            greet(device(col, place, col))
+
+        @pl.when(jnp.logical_not(lower))
+        def _():
+            for slot in range(row_groups):
+                greet(device(col, slot, col))
+            greet(device(group, place, group))
+
+    pl.semaphore_wait(
+        barrier,
+        jnp.where(inside, row_groups - 1 + (col_count - 1) * (row_groups + 1), row_groups + 1),
+    )
+
+    def near(slot, at):
+        return remote(
+            block(slot), landed.at[at], send_sem.at[slot], recv_sem.at[at], device(group, slot, col)
+        )
+
+    def by_group(index, at):
+        return remote(
+            block(index),
+            group_relay.at[at, index],
+            send_sem.at[index],
+            group_recv.at[at, index],
+            device(col, place, col),
+        )
+
+    def by_col(index, at):
+        return remote(
+            block(half + index),
+            col_relay.at[at, index],
+            send_sem.at[half + index],
+            col_recv.at[at, index],
+            device(group, place, group),
+        )
+
+    def pass_group(index, other):
+        return remote(
+            group_relay.at[other, index],
+            landed.at[place],
+            group_send.at[other, index],
+            recv_sem.at[place],
+            device(group, index, other),
+        )
+
+    def pass_col(index, other):
+        return remote(
+            col_relay.at[other, index],
+            landed.at[place],
+            col_send.at[other, index],
+            recv_sem.at[place],
+            device(other, half + index, col),
+        )
+
+    @pl.when(jnp.logical_not(inside))
+    def _():
+        for index in range(half):
+            by_group(index, group).start()
+            by_col(index, col).start()
+        for slot in range(row_groups):
+            remote(
+                block(slot),
+                landed.at[slot],
+                send_sem.at[slot],
+                recv_sem.at[slot],
+                device(col, place, col),
+            ).wait_recv()
+        for index in range(half):
+            by_group(index, group).wait_send()
+            by_col(index, col).wait_send()
+
+    @pl.when(inside)
+    def _():
+        for step in range(1, row_groups):
+            near(near_slot(step), place).start()
+        local = pltpu.make_async_copy(block(place), landed.at[place], own_sem)
         local.start()
+        for index in range(half):
+            for other in others():
+                remote(
+                    block(index),
+                    group_relay.at[other, index],
+                    send_sem.at[index],
+                    group_recv.at[other, index],
+                    device(other, place, col),
+                ).wait_recv()
+                pass_group(index, other).start()
+                remote(
+                    block(index),
+                    col_relay.at[other, index],
+                    send_sem.at[index],
+                    col_recv.at[other, index],
+                    device(group, place, other),
+                ).wait_recv()
+                pass_col(index, other).start()
         local.wait()
-
-    for turn in range(row_groups):
-        slot = lax.rem(mine + turn, row_groups)
-
-        @pl.when(remote(slot))
-        def _():
-            arrival(slot).wait_recv()
-            copy(slot).wait_send()
+        for step in range(1, row_groups):
+            near(near_slot(step), near_slot(step)).wait_recv()
+            near(near_slot(step), place).wait_send()
+        for index in range(half):
+            for other in others():
+                pass_group(index, other).wait_send()
+                pass_col(index, other).wait_send()
 
     parts, lanes = landed.shape[1], landed.shape[3]
     each = lanes // rows_tile
@@ -232,14 +513,44 @@
     slab = sequences // 2
     f32, bf16 = jnp.float32, jnp.bfloat16
 
-    left = lax.all_gather(
-        jnp.transpose(first_homolog_embedding, (1, 2, 0)), "col", axis=0, tiled=True
-    ).reshape(rows_tile * width, sequences)
-    right = lax.all_gather(
-        jnp.transpose(second_homolog_embedding, (1, 2, 0)), ("row", "col"), axis=0, tiled=True
+    vmem = pl.BlockSpec(memory_space=pltpu.VMEM)
+    blocks = row_groups * col_count
+    dma = pltpu.SemaphoreType.DMA
+    left, right = pl.pallas_call(
+        functools.partial(gather_kernel, row_groups, col_count),
+        in_specs=[vmem, vmem],
+        out_specs=[vmem, vmem],
+        out_shape=[
+            jax.ShapeDtypeStruct((col_count, tokens_local * width, sequences), bf16),
+            jax.ShapeDtypeStruct((blocks, width * tokens_local, sequences), bf16),
+        ],
+        scratch_shapes=[
+            pltpu.VMEM((col_count, width * tokens_local, sequences), bf16),
+            dma((col_count,)),
+            dma((col_count,)),
+            dma((col_count,)),
+            dma((col_count,)),
+            dma((col_count,)),
+            dma((col_count,)),
+            dma((row_groups,)),
+            dma((row_groups,)),
+            dma((row_groups,)),
+            dma((row_groups,)),
+            dma((3,)),
+        ],
+        compiler_params=pltpu.CompilerParams(
+            collective_id=1, has_side_effects=True, vmem_limit_bytes=VMEM_BYTES
+        ),
+        name="gather_tokens",
+    )(
+        jnp.transpose(first_homolog_embedding, (1, 2, 0)).reshape(tokens_local * width, sequences),
+        jnp.transpose(second_homolog_embedding, (2, 1, 0)).reshape(width * tokens_local, sequences),
     )
-    right = lax.dynamic_slice_in_dim(right, col_at * cols_tile, cols_tile, 0)
-    right = jnp.transpose(right, (1, 0, 2))
+    left = left.reshape(rows_tile * width, sequences)
+    if tokens_local % 16:
+        right = jnp.transpose(
+            right.reshape(blocks, width, tokens_local, sequences), (1, 0, 2, 3)
+        ).reshape(1, width * cols_tile, sequences)
 
     chain_rows = lax.dynamic_slice_in_dim(token_chain_index, row_at * rows_tile, rows_tile, 0)
     chain_cols = lax.dynamic_slice_in_dim(token_chain_index, col_at * cols_tile, cols_tile, 0)
@@ -265,7 +576,7 @@
             pl.BlockSpec(memory_space=pltpu.SMEM),
             whole(cols_tile, sequences),
             pl.BlockSpec((group * width, sequences), lambda step: (step, 0)),
-            whole(width, cols_tile, sequences),
+            whole(*right.shape),
             pl.BlockSpec((group, cols_tile, channels), lambda step: (step, 0, 0)),
             whole(channels, width * width),
             whole(channels, cols_tile),
@@ -306,17 +617,23 @@
         distogram_weight.T,
     )
 
-    vmem = pl.BlockSpec(memory_space=pltpu.VMEM)
+    half = row_groups // 2
     logits = pl.pallas_call(
-        functools.partial(exchange_kernel, row_groups, rows_tile),
+        functools.partial(exchange_kernel, row_groups, col_count, rows_tile),
         in_specs=[vmem, vmem, pl.BlockSpec(memory_space=pltpu.SMEM)],
         out_specs=vmem,
         out_shape=jax.ShapeDtypeStruct((bins_count, rows_tile, cols_tile), f32),
         scratch_shapes=[
             pltpu.VMEM((row_groups, parts, rows_tile, lanes), bf16),
-            pltpu.SemaphoreType.DMA((row_groups,)),
-            pltpu.SemaphoreType.DMA((row_groups,)),
-            pltpu.SemaphoreType.DMA,
+            pltpu.VMEM((col_count, half, parts, rows_tile, lanes), bf16),
+            pltpu.VMEM((col_count, half, parts, rows_tile, lanes), bf16),
+            dma((row_groups,)),
+            dma((row_groups,)),
+            dma((col_count, half)),
+            dma((col_count, half)),
+            dma((col_count, half)),
+            dma((col_count, half)),
+            dma,
         ],
         compiler_params=pltpu.CompilerParams(
             collective_id=0, has_side_effects=True, vmem_limit_bytes=VMEM_BYTES

time: 198 us -> 140 us (0.71)
  the two profiles are of different devices: /device:TPU:19 before, /device:TPU:7 now
where the time goes in v2:
time: 140 us
  Pallas kernels  124 us (89%)
  local copies, waits for them, and re-layouts  15.1 us (11%)
    pallas_call x1, Pallas kernels, per_device(): pl.pallas_call(functools.partial(exchange_kernel, row_groups, col_count,...  50.9 us
    pallas_call x1, Pallas kernels, per_device(): pl.pallas_call(functools.partial(pair_kernel, slab, width, group, rows_ti...  41.7 us
    pallas_call x1, Pallas kernels, per_device(): pl.pallas_call(functools.partial(gather_kernel, row_groups, col_count), i...  30.9 us
    unnamed x6, local copies, waits for them, and re-layouts  6.86 us

profile of v2, /device:TPU:7, one launch (start us, length us, event | category | flops | bytes accessed | tf_op | source)
XLA Modules:
  0.0 140.1 jit_solution(8566541088408644807)
XLA Ops:
  0.6 0.0 copy-start
  0.6 1.3 dynamic_slice.6.chain_rows
  2.0 0.8 dynamic_slice.7
  2.7 0.8 broadcast_in_dim.6.chain_cols
  3.5 1.6 %copy.24 = bf16[32,16,128]{2,1,0:T(8,128)(2,1)} copy(bf16[32,16,128]{2,0,1:T(8,128)(2,1)} %bitcast.21) | data formatting | bytes 262144 | tf_op jit(solution)/shard_map/transpose | solution.py:547
  5.1 1.4 broadcast_in_dim.7.bias
  6.5 1.4 broadcast_in_dim.8.gain
  7.9 1.0 copy.26
  8.9 1.0 copy.27
  9.9 0.7 pad_maximum_fusion.gate_up
  10.7 1.6 %copy.28 = bf16[512,128]{0,1:T(8,128)(2,1)} copy(bf16[512,128]{1,0:T(8,128)(2,1)} %param.21) | data formatting | bytes 262144 | tf_op args[9]
  12.3 0.0 copy-done
  12.3 0.1 copy.25
  12.4 0.9 copy.29.mixing
  13.3 30.9 %gather_tokens.1 = (bf16[2,512,128]{2,1,0:T(8,128)(2,1)}, bf16[16,512,128]{2,1,0:T(8,128)(2,1)}) custom-call(bf16[512,128]{1,0:T(8,128)(2,1)} %bitcast.22, bf16[512,128]{1,0:T(8,128)(2,1)} %bitcast.16), custom_call_target="tpu_custom_call" | custom-call | tf_op jit(solution)/shard_map/gather_tokens/pallas_call | solution.py:519
  44.2 41.7 %pair_tile.1 = (bf16[32,256,128]{2,1,0:T(8,128)(2,1)}, bf16[64,32,256]{2,1,0:T(8,128)(2,1)}, bf16[16,256,128]{2,1,0:T(8,128)(2,1)}) custom-call(s32[32]{0:T(128)} %dynamic_slice.6.chain_rows, s32[256,128]{1,0:T(8,128)} %broadcast_in_dim.6.chain_cols, bf16[1024,128]{1,0:T(8,128)(2,1)} %bitcast.19, bf16[16,512,128]{2,1,0:T(8,128)(2,1)} %get-tuple-element.8.right, ...), custom_call_target="tpu_custom_call" | custom-call | tf_op jit(solution)/shard_map/pair_tile/pallas_call | solution.py:572
  86.0 50.9 %mirror_bins.1 = f32[64,32,256]{2,1,0:T(8,128)} custom-call(bf16[16,256,128]{2,1,0:T(8,128)(2,1)} %get-tuple-element.10.turned_bins, bf16[64,32,256]{2,1,0:T(8,128)(2,1)} %get-tuple-element.11.own_bins, f32[64]{0:T(128)} %bias.1), custom_call_target="tpu_custom_call" | custom-call | tf_op jit(solution)/shard_map/mirror_bins/pallas_call | solution.py:621
  136.9 3.2 %copy.31 = f32[64,32,256]{2,1,0:T(8,128)} copy(f32[64,32,256]{2,1,0:T(8,128)} %mirror_bins.1) | data formatting | bytes 4194304
Async XLA Ops:
  0.6 11.7 %copy-start = (bf16[1024,128]{1,0:T(8,128)(2,1)S(1)}, bf16[1024,128]{1,0:T(8,128)(2,1)}, u32[]{:S(2)}) copy-start(bf16[1024,128]{1,0:T(8,128)(2,1)} %param.16) | copy-start | bytes 786436

commit v3 on v2

--- a/solution.py
+++ b/solution.py
@@ -16,17 +16,18 @@
     width,
     group,
     rows_tile,
-    chain_rows,
-    chain_cols,
+    chain_all,
+    chain_line,
     left,
     right,
     incoming,
     mixing,
-    bias,
-    gain,
-    gate_up,
-    down,
-    bins_weight,
+    bias_line,
+    gain_line,
+    gate_weight,
+    up_weight,
+    down_weight,
+    bins_weight_in,
     pair_out,
     own_bins,
     turned_bins,
@@ -34,6 +35,12 @@
     weights,
     outer,
     bins,
+    chain_cols,
+    bias,
+    gain,
+    gate_up,
+    down,
+    bins_weight,
 ):
     step = pl.program_id(0)
     cols_tile = chain_cols.shape[0]
@@ -43,20 +50,36 @@
     bins_count = bins_weight.shape[0]
     sides, _, lanes = bins.shape
     first_row = step * group
-    first_chain = chain_rows[first_row]
-    last_chain = chain_rows[first_row + group - 1]
+    row_base = lax.axis_index("row") * rows_tile + first_row
+    first_chain = chain_all[row_base]
+    last_chain = chain_all[row_base + group - 1]
+
+    def turned(value):
+        return value.astype(jnp.float32).T
+
+    @pl.when(step == 0)
+    def _():
+        start = pl.multiple_of(lax.axis_index("col") * cols_tile, cols_tile)
+        line = chain_line[:, pl.ds(start, cols_tile)].astype(jnp.float32)
+        chain_cols[...] = jnp.broadcast_to(line, (sequences, cols_tile)).T
+        bias[...] = jnp.broadcast_to(bias_line[...], (cols_tile, channels)).T
+        gain[...] = jnp.broadcast_to(gain_line[...], (cols_tile, channels)).T
+        gate_up[:hid] = turned(gate_weight[...]).astype(jnp.bfloat16)
+        gate_up[hid:] = turned(up_weight[...]).astype(jnp.bfloat16)
+        down[...] = turned(down_weight[...]).astype(jnp.bfloat16)
+        bins_weight[...] = turned(bins_weight_in[...]).astype(jnp.bfloat16)
 
     def load_chains(low):
         lane = lax.broadcasted_iota(jnp.int32, (cols_tile, sequences), 1)
         apart = jnp.where(lane < slab, 1.0 / slab, 0.0).astype(jnp.float32)
         for half in range(2):
             chain = low + half
-            same = chain_cols[...] == chain
+            same = chain_cols[...] == chain.astype(jnp.float32)
             weights[:, half * sequences : (half + 1) * sequences] = jnp.where(
                 same, 0.5 / slab, apart
             ).astype(jnp.bfloat16)
             for row in range(group):
-                keep = jnp.where(chain_rows[first_row + row] == chain, 1.0, 0.0)
+                keep = jnp.where(chain_all[row_base + row] == chain, 1.0, 0.0)
                 lhs[row * width : (row + 1) * width, half * sequences : (half + 1) * sequences] = (
                     left[row * width : (row + 1) * width, :].astype(jnp.float32) * keep
                 ).astype(jnp.bfloat16)
@@ -297,9 +320,6 @@
     col_count,
     rows_tile,
     turned_bins,
-    own_bins,
-    bias,
-    logits,
     landed,
     group_relay,
     col_relay,
@@ -442,10 +462,10 @@
 
     @pl.when(inside)
     def _():
+        local = pltpu.make_async_copy(block(place), landed.at[place], own_sem)
+        local.start()
         for step in range(1, row_groups):
             near(near_slot(step), place).start()
-        local = pltpu.make_async_copy(block(place), landed.at[place], own_sem)
-        local.start()
         for index in range(half):
             for other in others():
                 remote(
@@ -473,8 +493,10 @@
                 pass_group(index, other).wait_send()
                 pass_col(index, other).wait_send()
 
-    parts, lanes = landed.shape[1], landed.shape[3]
+def add_kernel(own_bins, landed, bias, logits):
+    row_groups, parts, rows_tile, lanes = landed.shape
     each = lanes // rows_tile
+    first = pl.program_id(0) * parts * each
 
     @pl.loop(0, parts)
     def _(part):
@@ -484,7 +506,7 @@
                 [one[:, inner * rows_tile : (inner + 1) * rows_tile] for one in got], axis=1
             )
             at = part * each + inner
-            logits[at] = own_bins[at].astype(jnp.float32) + mirrored + bias[at]
+            logits[at] = own_bins[at].astype(jnp.float32) + mirrored + bias[first + at]
 
 
 def per_device(
@@ -503,8 +525,6 @@
 ):
     row_count = lax.axis_size("row")
     col_count = lax.axis_size("col")
-    row_at = lax.axis_index("row")
-    col_at = lax.axis_index("col")
     rows_tile, cols_tile, channels = incoming_pair_state.shape
     sequences, tokens_local, width = first_homolog_embedding.shape
     hid = transition_gate_weight.shape[1]
@@ -552,16 +572,9 @@
             right.reshape(blocks, width, tokens_local, sequences), (1, 0, 2, 3)
         ).reshape(1, width * cols_tile, sequences)
 
-    chain_rows = lax.dynamic_slice_in_dim(token_chain_index, row_at * rows_tile, rows_tile, 0)
-    chain_cols = lax.dynamic_slice_in_dim(token_chain_index, col_at * cols_tile, cols_tile, 0)
-    chain_cols = jnp.broadcast_to(chain_cols[:, None], (cols_tile, sequences))
     mixing = jnp.transpose(
         tensor_mixing_matrix.reshape(width, width, channels), (2, 1, 0)
     ).reshape(channels, width * width)
-    bias = jnp.broadcast_to(outer_product_bias[:, None], (channels, cols_tile))
-    gain = jnp.broadcast_to(transition_norm_gain[:, None], (channels, cols_tile))
-    gate_up = jnp.concatenate([transition_gate_weight.T, transition_up_weight.T], axis=0)
-
     group = min(16, rows_tile)
     lanes = 128
     parts = bins_count * rows_tile // lanes
@@ -574,16 +587,17 @@
         grid=(rows_tile // group,),
         in_specs=[
             pl.BlockSpec(memory_space=pltpu.SMEM),
-            whole(cols_tile, sequences),
+            whole(1, token_chain_index.shape[0]),
             pl.BlockSpec((group * width, sequences), lambda step: (step, 0)),
             whole(*right.shape),
             pl.BlockSpec((group, cols_tile, channels), lambda step: (step, 0, 0)),
             whole(channels, width * width),
-            whole(channels, cols_tile),
-            whole(channels, cols_tile),
-            whole(2 * hid, channels),
+            whole(1, channels),
+            whole(1, channels),
             whole(channels, hid),
-            whole(bins_count, channels),
+            whole(channels, hid),
+            whole(hid, channels),
+            whole(channels, bins_count),
         ],
         out_specs=[
             pl.BlockSpec((group, cols_tile, channels), lambda step: (step, 0, 0)),
@@ -600,31 +614,37 @@
             pltpu.VMEM((cols_tile, 2 * sequences), bf16),
             pltpu.VMEM((group, width * width, cols_tile), bf16),
             pltpu.VMEM((cols_tile // lanes, bins_count * rows_tile, lanes), f32),
+            pltpu.VMEM((cols_tile, sequences), f32),
+            pltpu.VMEM((channels, cols_tile), f32),
+            pltpu.VMEM((channels, cols_tile), f32),
+            pltpu.VMEM((2 * hid, channels), bf16),
+            pltpu.VMEM((channels, hid), bf16),
+            pltpu.VMEM((bins_count, channels), bf16),
         ],
         compiler_params=pltpu.CompilerParams(vmem_limit_bytes=VMEM_BYTES),
         name="pair_tile",
     )(
-        chain_rows,
-        chain_cols,
+        token_chain_index,
+        token_chain_index[None, :],
         left,
         right,
         incoming_pair_state,
         mixing,
-        bias,
-        gain,
-        gate_up,
-        transition_down_weight.T,
-        distogram_weight.T,
+        outer_product_bias[None, :],
+        transition_norm_gain[None, :],
+        transition_gate_weight,
+        transition_up_weight,
+        transition_down_weight,
+        distogram_weight,
     )
 
     half = row_groups // 2
-    logits = pl.pallas_call(
+    landed = pl.pallas_call(
         functools.partial(exchange_kernel, row_groups, col_count, rows_tile),
-        in_specs=[vmem, vmem, pl.BlockSpec(memory_space=pltpu.SMEM)],
+        in_specs=[vmem],
         out_specs=vmem,
-        out_shape=jax.ShapeDtypeStruct((bins_count, rows_tile, cols_tile), f32),
+        out_shape=jax.ShapeDtypeStruct((row_groups, parts, rows_tile, lanes), bf16),
         scratch_shapes=[
-            pltpu.VMEM((row_groups, parts, rows_tile, lanes), bf16),
             pltpu.VMEM((col_count, half, parts, rows_tile, lanes), bf16),
             pltpu.VMEM((col_count, half, parts, rows_tile, lanes), bf16),
             dma((row_groups,)),
@@ -639,7 +659,25 @@
             collective_id=0, has_side_effects=True, vmem_limit_bytes=VMEM_BYTES
         ),
         name="mirror_bins",
-    )(turned_bins, own_bins, distogram_bias)
+    )(turned_bins)
+    steps = 4
+    logits = pl.pallas_call(
+        add_kernel,
+        grid=(steps,),
+        in_specs=[
+            pl.BlockSpec((bins_count // steps, rows_tile, cols_tile), lambda step: (step, 0, 0)),
+            pl.BlockSpec(
+                (row_groups, parts // steps, rows_tile, lanes), lambda step: (0, step, 0, 0)
+            ),
+            pl.BlockSpec(memory_space=pltpu.SMEM),
+        ],
+        out_specs=pl.BlockSpec(
+            (bins_count // steps, rows_tile, cols_tile), lambda step: (step, 0, 0)
+        ),
+        out_shape=jax.ShapeDtypeStruct((bins_count, rows_tile, cols_tile), f32),
+        compiler_params=pltpu.CompilerParams(vmem_limit_bytes=VMEM_BYTES),
+        name="add_bins",
+    )(own_bins, landed, distogram_bias)
     return (pair_out, logits)
 
 

time: 140 us -> 134 us (0.957); the launches traced: 140 us -> 136 us
  local copies, waits for them, and re-layouts: 15.1 us -> 4.94 us
  Pallas kernels: 124 us -> 130 us
    unnamed x6 -> x1, local copies, waits for them, and re-layouts: 6.86 us -> 1.42 us
    pallas_call x0 -> x1, Pallas kernels: none -> 4.72 us  [per_device(): pl.pallas_call(add_kernel, grid=(steps,), in_specs=[pl.BlockSpec((bins_co...]
    broadcast_in_dim x3 -> x0, local copies, waits for them, and re-layouts: 3.54 us -> none  [the longest x1 1.4 us: per_device(): bias = jnp.broadcast_to(outer_product_bias[:, None], (channels, cols_tile))]
    dynamic_slice x2 -> x0, local copies, waits for them, and re-layouts: 2.07 us -> none  [the longest x1 1.32 us: per_device(): lax.dynamic_slice_in_dim(token_chain_index, row_at * rows_tile, rows_tile...]
    pallas_call x1, Pallas kernels: 50.9 us -> 52.8 us  [per_device(): pl.pallas_call(functools.partial(exchange_kernel, row_groups, col_count,...]
where the time goes in v3:
time: 134 us; the launch traced here: 136 us
  Pallas kernels  130 us (97%)
  local copies, waits for them, and re-layouts  4.94 us (4%)
    pallas_call x1, Pallas kernels, per_device(): pl.pallas_call(functools.partial(exchange_kernel, row_groups, col_count,...  52.8 us
    pallas_call x1, Pallas kernels, per_device(): pl.pallas_call(functools.partial(pair_kernel, slab, width, group, rows_ti...  41.9 us
    pallas_call x1, Pallas kernels, per_device(): pl.pallas_call(functools.partial(gather_kernel, row_groups, col_count), i...  31 us
    pallas_call x1, Pallas kernels, per_device(): pl.pallas_call(add_kernel, grid=(steps,), in_specs=[pl.BlockSpec((bins_co...  4.72 us

profile of v3, /device:TPU:7, one launch (start us, length us, event | category | flops | bytes accessed | tf_op | source)
XLA Modules:
  0.0 136.0 jit_solution(5277474896829597145)
XLA Ops:
  0.6 1.4 %copy.23.bins_weight_in = bf16[128,64]{1,0:T(8,128)(2,1)} copy(bf16[128,64]{0,1:T(8,128)(2,1)} %param.22) | data formatting | bytes 32768 | tf_op args[10]
  2.1 1.6 %copy.20 = bf16[32,16,128]{2,1,0:T(8,128)(2,1)} copy(bf16[32,16,128]{2,0,1:T(8,128)(2,1)} %bitcast.17) | data formatting | bytes 262144 | tf_op jit(solution)/shard_map/transpose | solution.py:567
  3.7 1.1 copy.21
  4.7 0.8 copy.22.mixing
  5.6 31.0 %gather_tokens.1 = (bf16[2,512,128]{2,1,0:T(8,128)(2,1)}, bf16[16,512,128]{2,1,0:T(8,128)(2,1)}) custom-call(bf16[512,128]{1,0:T(8,128)(2,1)} %bitcast.18, bf16[512,128]{1,0:T(8,128)(2,1)} %bitcast.14), custom_call_target="tpu_custom_call" | custom-call | tf_op jit(solution)/shard_map/gather_tokens/pallas_call | solution.py:539
  36.5 41.9 %pair_tile.1 = (bf16[32,256,128]{2,1,0:T(8,128)(2,1)}, bf16[64,32,256]{2,1,0:T(8,128)(2,1)}, bf16[16,256,128]{2,1,0:T(8,128)(2,1)}) custom-call(s32[512]{0:T(512)} %chain_all.1, s32[1,512]{1,0:T(1,128)} %bitcast.19, bf16[1024,128]{1,0:T(8,128)(2,1)} %bitcast.15, bf16[16,512,128]{2,1,0:T(8,128)(2,1)} %get-tuple-element.8.right, ...), custom_call_target="tpu_custom_call" | custom-call | tf_op jit(solution)/shard_map/pair_tile/pallas_call | solution.py:585
  78.5 52.8 %mirror_bins.1.landed = bf16[8,16,32,128]{3,2,1,0:T(8,128)(2,1)} custom-call(bf16[16,256,128]{2,1,0:T(8,128)(2,1)} %get-tuple-element.11.turned_bins), custom_call_target="tpu_custom_call" | custom-call | tf_op jit(solution)/shard_map/mirror_bins/pallas_call | solution.py:642
  131.3 4.7 %add_bins.1 = f32[64,32,256]{2,1,0:T(8,128)} custom-call(bf16[64,32,256]{2,1,0:T(8,128)(2,1)} %get-tuple-element.10.own_bins, bf16[8,16,32,128]{3,2,1,0:T(8,128)(2,1)} %mirror_bins.1.landed, f32[64]{0:T(128)} %bias.1), custom_call_target="tpu_custom_call" | custom-call | tf_op jit(solution)/shard_map/add_bins/pallas_call | solution.py:664
